TPU v7x, 128 devices: a whole 4x4x4 slice. The times are simulated.
128 devices in a mesh: lat: 4 (over y_hi, core), lon: 32 (over x, y_lo, z).
Axes of the slice: x: 4, y: 4 (y_hi: 2, y_lo: 2; y = y_hi * 2 + y_lo), z: 4, core: 2. Of those that a mesh axis runs over, the one named last changes fastest.
Arguments:
- tokens: bfloat16 [4, 8, 48, 384, 384], P(None, None, 'lat', 'lon'), may hold values from -6 to 6
- w_qkv: bfloat16 [384, 1152], replicated, may hold values from -0.3125 to 0.3125
- w_proj: bfloat16 [384, 384], replicated, may hold values from -0.3125 to 0.3125
- w_up: bfloat16 [384, 1536], replicated, may hold values from -0.3125 to 0.3125
- w_down: bfloat16 [1536, 384], replicated, may hold values from -0.15625 to 0.15625
- w_merge: bfloat16 [1536, 768], replicated, may hold values from -0.15625 to 0.15625
- earth_bias: float32 [8, 4, 3312, 12], P('lat'), may hold values from -3 to 303
- position_index: int32 [144, 144], replicated, may hold values from 0 to 3311
- region_ids: int32 [8, 4, 144], P('lat'), may hold values from 0 to 2
Outputs:
- merged: bfloat16 [4, 8, 24, 192, 768], P(None, None, 'lat', 'lon')
All inputs are finite; a program needn't handle non-finite values.
Results may differ from a plain program's by a relative error of at most 0.019.
Values may be sent and summed in bfloat16 or wider, within the bound.
A program may use at most 192 MiB of HBM per device.

v0:
```python
import jax
import jax.numpy as jnp
import numpy as np
from jax import lax
from jax.experimental import pallas as pl
from jax.experimental.pallas import tpu as pltpu
from jax.sharding import PartitionSpec as P

HEADS = 12
HEAD_DIM = 32
C = 384
FFN = 1536
ZL = 8
ZW = 4
HALF = 72
SLOTS = 144
LANES = 256
CELLS = 288
PIECE = 144
LOG2E = 1.4426950408889634
BF = jnp.bfloat16
F32 = jnp.float32


def passed_along(block, axis, distance):
    devices = range(lax.axis_size(axis))
    route = [((i - distance) % len(devices), i) for i in devices]
    return lax.ppermute(block, axis, route)


def window_order():
    one_hot = np.zeros((CELLS, CELLS), np.float32)
    for zw in range(ZW):
        for z in range(2):
            for r in range(6):
                for c in range(6):
                    one_hot[zw * HALF + z * 36 + r * 6 + c, (r * 6 + c) * ZL + (2 * zw + 1 + z) % ZL] = 1.0
    return one_hot


def normalized(x):
    width = x.shape[-1]
    center = x - jnp.sum(x, axis=-1, keepdims=True) * (1.0 / width)
    spread = jnp.sum(center * center, axis=-1, keepdims=True) * (1.0 / width)
    return center * lax.rsqrt(spread + 1e-05)


def dot(a, b):
    return jnp.dot(a, b, preferred_element_type=F32)


def neighbour(axis, distance):
    size = lax.axis_size(axis)
    return {axis: lax.rem(lax.axis_index(axis) + distance + size, size)}


def remote(source, target, send_sem, recv_sem, axis, distance):
    return pltpu.make_async_remote_copy(
        src_ref=source,
        dst_ref=target,
        send_sem=send_sem,
        recv_sem=recv_sem,
        device_id=neighbour(axis, distance),
        device_id_type=pl.DeviceIdType.MESH,
    )


def greet(axes):
    barrier = pltpu.get_barrier_semaphore()
    for axis in axes:
        for distance in (-1, 1):
            pl.semaphore_signal(
                barrier, inc=1, device_id=neighbour(axis, distance), device_id_type=pl.DeviceIdType.MESH
            )


def greeted(axes):
    pl.semaphore_wait(pltpu.get_barrier_semaphore(), 2 * len(axes))


def full(shape):
    return pl.BlockSpec(shape, lambda *i: (0,) * len(shape))


ROWS_AT_ONCE = 8
STEPS = SLOTS // ROWS_AT_ONCE
TYPE_HEADS = 96
PITCH = 97
TABLE = 3312
ALONG = 4
FORWARD = 10
PICKS = 4


def slot_order():
    return np.arange(SLOTS, dtype=np.int32).reshape(12, 2, 6).transpose(1, 0, 2).reshape(-1)


def gather_kernel(
    index_ref, tok_ref, table_ref, labels_ref, slots_ref,
    out_ref, mid_left, mid_right, last_left, last_right, below_left, below_right,
    next_last, prev_last, next_below, prev_below,
    rows, picked, left, right, region_ref, region_col_ref, mids, firsts, lasts, send_sems, recv_sems, local_sems,
):
    step = pl.program_id(0)

    routes = (
        (firsts.at[0], below_left, "lat", -1),
        (firsts.at[1], below_right, "lat", -1),
        (lasts.at[0], next_last, "lon", -1),
        (lasts.at[1], prev_last, "lon", 1),
        (below_left, next_below, "lon", -1),
        (below_right, prev_below, "lon", 1),
    )

    def block(n):
        source, target, axis, distance = routes[n]
        return remote(source, target, send_sems.at[n], recv_sems.at[n], axis, distance)

    def local():
        pairs = (
            (mids.at[0], mid_left), (mids.at[1], mid_right), (lasts.at[0], last_left), (lasts.at[1], last_right)
        )
        return [pltpu.make_async_copy(a, b, local_sems.at[n]) for n, (a, b) in enumerate(pairs)]

    @pl.when(step == 0)
    def _():
        greet(("lat", "lon"))
        for piece, blocks in ((0, (firsts,)), (3, (lasts,)), (1, (mids, 0)), (2, (mids, 1))):
            for b in range(tok_ref.shape[0]):
                x = normalized(tok_ref[b, 3 * piece : 3 * piece + 3].astype(F32))
                for side in range(2):
                    part = x[:, 6 * side : 6 * side + 6].reshape(PIECE, C).astype(BF)
                    if len(blocks) == 1:
                        blocks[0][side, b] = part
                    else:
                        blocks[0][side, b, blocks[1]] = part
            if piece == 0:
                greeted(("lat", "lon"))
                block(0).start()
                block(1).start()
        for copy in local():
            copy.start()
        for c in range(0, TABLE, 128):
            width = min(128, TABLE - c)
            some = table_ref[:, :, :, c : c + width].reshape(TYPE_HEADS, width)
            rows[c : c + width, :TYPE_HEADS] = some.T
        labels = dot((labels_ref[...] + 1).astype(F32).astype(BF), slots_ref[...])
        region_ref[...] = labels
        region_col_ref[...] = labels.T

    @pl.when(step == ALONG)
    def _():
        block(2).start()
        block(3).start()

    @pl.when(step == FORWARD)
    def _():
        for n in range(2):
            block(n).wait_recv()
            block(4 + n).start()

    def pick(turn, carry):
        for j in range(PICKS):
            row = step * ROWS_AT_ONCE + turn * (PICKS // 2) + j // 2
            side, place = row // HALF, row % HALF
            slot = (place // 6) * 12 + side * 6 + place % 6
            base = pl.multiple_of(turn * (PICKS * HALF) + j * HALF, 8)
            for k in range(HALF):
                picked[pl.ds(base + k, 1), :] = rows[pl.ds(index_ref[slot, j % 2 * 6 + k // 6 * 12 + k % 6], 1), :]
        return carry

    lax.fori_loop(0, ROWS_AT_ONCE * 2 // PICKS, pick, 0)
    for s in range(ROWS_AT_ONCE):
        left[PITCH * s : PITCH * s + TYPE_HEADS, :] = picked[SLOTS * s : SLOTS * s + 128, :].T[:TYPE_HEADS]
        right[PITCH * s : PITCH * s + TYPE_HEADS, :16] = picked[SLOTS * s + 128 : SLOTS * (s + 1), :].T[:TYPE_HEADS]
    for lw in range(2):
        for zw in range(ZW):
            kind = lw * ZW + zw
            same = region_col_ref[pl.ds(pl.multiple_of(step * ROWS_AT_ONCE, 8), ROWS_AT_ONCE), kind : kind + 1] == region_ref[kind : kind + 1, :]
            for h in range(HEADS):
                source = (lw * HEADS + h) * ZW + zw
                place = kind * HEADS + h
                out_ref[0, place, :, :128] = jnp.where(
                    same[:, :128], left[pl.ds(source, ROWS_AT_ONCE, stride=PITCH), :] * LOG2E, -1e9
                )
                out_ref[0, place, :, 128:] = jnp.where(
                    same[:, 128:], right[pl.ds(source, ROWS_AT_ONCE, stride=PITCH), :] * LOG2E, -1e9
                )

    @pl.when(step == STEPS - 1)
    def _():
        for n in range(6):
            block(n).wait_send()
            if n >= 2:
                block(n).wait_recv()
        for copy in local():
            copy.wait()


def gather(tok, earth_bias, position_index, region_ids):
    batch = tok.shape[0]
    table = jnp.transpose(earth_bias, (0, 3, 1, 2))
    slots = np.zeros((SLOTS, LANES), np.float32)
    slots[slot_order(), np.arange(SLOTS)] = 1.0
    two, one = jax.ShapeDtypeStruct((batch, 2, PIECE, C), BF), jax.ShapeDtypeStruct((batch, PIECE, C), BF)
    anywhere = pl.BlockSpec(memory_space=pl.ANY)
    return pl.pallas_call(
        gather_kernel,
        grid=(STEPS,),
        in_specs=[
            pl.BlockSpec(memory_space=pltpu.SMEM),
            full(tok.shape),
            full(table.shape),
            full((2 * ZW, SLOTS)),
            full((SLOTS, LANES)),
        ],
        out_specs=[pl.BlockSpec((1, TYPE_HEADS, ROWS_AT_ONCE, LANES), lambda i: (i, 0, 0, 0))] + [anywhere] * 10,
        out_shape=[jax.ShapeDtypeStruct((STEPS, TYPE_HEADS, ROWS_AT_ONCE, LANES), F32)]
        + [two, two] + [one] * 8,
        scratch_shapes=[
            pltpu.VMEM((TABLE, 128), F32),
            pltpu.VMEM((ROWS_AT_ONCE * SLOTS, 128), F32),
            pltpu.VMEM((ROWS_AT_ONCE * PITCH, 128), F32),
            pltpu.VMEM((ROWS_AT_ONCE * PITCH, 128), F32),
            pltpu.VMEM((2 * ZW, LANES), F32),
            pltpu.VMEM((LANES, 2 * ZW), F32),
            pltpu.VMEM((2, batch, 2, PIECE, C), BF),
            pltpu.VMEM((2, batch, PIECE, C), BF),
            pltpu.VMEM((2, batch, PIECE, C), BF),
            pltpu.SemaphoreType.DMA((6,)),
            pltpu.SemaphoreType.DMA((6,)),
            pltpu.SemaphoreType.DMA((4,)),
        ],
        cost_estimate=pl.CostEstimate(flops=20_000_000, bytes_accessed=100_000_000, transcendentals=0),
        compiler_params=pltpu.CompilerParams(
            collective_id=0, has_side_effects=True, vmem_limit_bytes=60 << 20
        ),
        name="gather",
    )(position_index, tok, table, region_ids.reshape(2 * ZW, SLOTS), jnp.asarray(slots, BF))


def attend_kernel(
    lower_a, lower_b, upper_a, upper_b, right_a, right_b, left_a, left_b, order_ref, back_ref, w_qkv_ref, w_proj_ref, *rest
):
    bias_refs, rest = rest[:2], rest[2:]
    if len(rest) > 5:
        mid_left, mid_right, out_a, out_b, next_mid, prev_mid, own_scr, halo_scr, ctx_scr, send_sems, recv_sems = rest

        def blocks():
            return (
                remote(mid_left, next_mid, send_sems.at[0], recv_sems.at[0], "lon", -1),
                remote(mid_right, prev_mid, send_sems.at[1], recv_sems.at[1], "lon", 1),
            )

        @pl.when(pl.program_id(0) == 0)
        def _():
            greet(("lon",))
            greeted(("lon",))
            for block in blocks():
                block.start()
    else:
        blocks = None
        out_a, out_b, own_scr, halo_scr, ctx_scr = rest
    order = order_ref[...]

    def windows(top, bottom):
        return dot(order, jnp.concatenate([top, bottom], axis=0)).astype(BF)

    own = jnp.concatenate([windows(upper_a[0], upper_b[0]), windows(lower_a[0], lower_b[0])], axis=0)
    own_scr[...] = dot(own, w_qkv_ref[...])
    halo = jnp.concatenate([windows(right_a[0], right_b[0]), windows(left_a[0], left_b[0])], axis=0)
    halo_scr[...] = dot(halo, w_qkv_ref[:, C:])
    lane_head = lax.broadcasted_iota(jnp.int32, (1, 128), 1) // HEAD_DIM
    masks = [lane_head == h for h in range(4)]
    ones = jnp.ones((SLOTS, 128), BF)

    for zw in range(ZW):
        for side in range(2):
            rows = slice(side * CELLS + zw * HALF, side * CELLS + (zw + 1) * HALF)
            for g in range(3):
                lanes = slice(128 * g, 128 * g + 128)
                klanes = slice(C + 128 * g, C + 128 * g + 128)
                vlanes = slice(2 * C + 128 * g, 2 * C + 128 * g + 128)
                q = own_scr[rows, lanes] * (HEAD_DIM ** (-0.5) * LOG2E)
                stacked = jnp.concatenate([jnp.where(m, q, 0.0) for m in masks], axis=0).astype(BF)
                k = [own_scr[rows, klanes], halo_scr[rows, lanes]]
                v = [own_scr[rows, vlanes], halo_scr[rows, klanes]]
                if side == 1:
                    k, v = k[::-1], v[::-1]
                keys = jnp.concatenate(k, axis=0).astype(BF)
                values = jnp.concatenate([jnp.concatenate(v, axis=0).astype(BF), ones], axis=1)
                scores = lax.dot_general(stacked, keys, (((1,), (1,)), ((), ())), preferred_element_type=F32)
                bias = jnp.swapaxes(bias_refs[side][:, zw * HEADS + 4 * g : zw * HEADS + 4 * g + 4, :, :SLOTS], 0, 1)
                scores = scores + bias.reshape(4 * HALF, SLOTS)
                raised = jnp.exp2(scores - jnp.max(scores, axis=-1, keepdims=True)).astype(BF)
                both = dot(raised, values)
                top, total = both[:HALF, :128], both[:HALF, 128:]
                for h in range(1, 4):
                    top = jnp.where(masks[h], both[h * HALF : (h + 1) * HALF, :128], top)
                    total = jnp.where(masks[h], both[h * HALF : (h + 1) * HALF, 128:], total)
                ctx_scr[rows, lanes] = top / total
    back = back_ref[...]
    for side in range(2):
        natural = dot(back, ctx_scr[CELLS * side : CELLS * (side + 1), :].astype(BF)).astype(BF)
        result = dot(natural, w_proj_ref[...]).astype(BF)
        out_a[1 - side, 0] = result[:PIECE]
        out_b[1 - side, 0] = result[PIECE:]
    if blocks is not None:

        @pl.when(pl.program_id(0) == pl.num_programs(0) - 1)
        def _():
            for block in blocks():
                block.wait()


def attend(streams, order, w_qkv, w_proj, bias, lw, travelling=()):
    batch = streams[-1][0].shape[0]
    arrays, specs = [], []
    for array, dim, index in streams:
        arrays.append(array)
        if dim is None:
            specs.append(pl.BlockSpec((1, PIECE, C), lambda b: (b, 0, 0)))
        elif dim == 0:
            specs.append(pl.BlockSpec((None, 1, PIECE, C), lambda b, i=index: (i, b, 0, 0)))
        else:
            specs.append(pl.BlockSpec((1, None, PIECE, C), lambda b, i=index: (b, i, 0, 0)))
    anywhere = [pl.BlockSpec(memory_space=pl.ANY)] * len(travelling)
    sems = [pltpu.SemaphoreType.DMA((2,))] * len(travelling)
    remote_params = dict(collective_id=1, has_side_effects=True) if travelling else {}
    out = jax.ShapeDtypeStruct((2, batch, PIECE, C), BF)
    out_spec = pl.BlockSpec((2, 1, PIECE, C), lambda b: (0, b, 0, 0))
    return pl.pallas_call(
        attend_kernel,
        grid=(batch,),
        in_specs=specs
        + [
            full((CELLS, CELLS)),
            full((CELLS, CELLS)),
            full((C, 3 * C)),
            full((C, C)),
            pl.BlockSpec((STEPS // 2, ZW * HEADS, ROWS_AT_ONCE, LANES), lambda b: (0, lw, 0, 0)),
            pl.BlockSpec((STEPS // 2, ZW * HEADS, ROWS_AT_ONCE, LANES), lambda b: (1, lw, 0, 0)),
        ]
        + anywhere,
        out_specs=[out_spec, out_spec] + anywhere,
        out_shape=[out, out] + [jax.ShapeDtypeStruct(array.shape, BF) for array in travelling],
        scratch_shapes=[
            pltpu.VMEM((2 * CELLS, 3 * C), F32),
            pltpu.VMEM((2 * CELLS, 2 * C), F32),
            pltpu.VMEM((2 * CELLS, C), F32),
        ]
        + sems,
        cost_estimate=pl.CostEstimate(flops=20_000_000_000, bytes_accessed=16_000_000, transcendentals=4_000_000),
        compiler_params=pltpu.CompilerParams(vmem_limit_bytes=60 << 20, **remote_params),
        name="attend",
    )(*arrays, jnp.asarray(order, BF), jnp.asarray(order.T, BF), w_qkv, w_proj, bias, bias, *travelling)


CHUNK = 768


def feed_kernel(tok_ref, first_ref, mid_a, mid_b, last_ref, w_up_ref, w_down_ref, w_merge_ref, out_ref, hidden_scr):
    for piece, ref in enumerate((first_ref, mid_a, mid_b, last_ref)):
        for side in range(2):
            rows, cols = slice(3 * piece, 3 * piece + 3), slice(6 * side, 6 * side + 6)
            tok = tok_ref[0, rows, cols].astype(F32)
            attended = ref[side, 0].astype(F32).reshape(3, 6, ZL, C)
            hidden_scr[rows, cols] = (tok + attended).astype(BF).astype(F32)

    hidden = hidden_scr[...].reshape(12 * 12 * ZL, C)
    normed = normalized(hidden).astype(BF)
    block = hidden
    for f in range(0, FFN, CHUNK):
        up = dot(normed, w_up_ref[:, f : f + CHUNK])
        inner = (0.5 * up * (1.0 + lax.erf(up * 0.7071067811865476))).astype(BF)
        block = block + dot(inner, w_down_ref[f : f + CHUNK])
    block = block.astype(BF).astype(F32).reshape(6, 2, 6, 2, ZL, C)
    grouped = jnp.concatenate([block[:, p // 2, :, p % 2] for p in range(4)], axis=-1)
    grouped = normalized(grouped.reshape(36 * ZL, 4 * C)).astype(BF)
    out_ref[0] = dot(grouped, w_merge_ref[...]).reshape(6, 6, ZL, 2 * C).astype(BF)


def feed(tok, first, mid_a, mid_b, last, w_up, w_down, w_merge):
    batch = tok.shape[0]
    piece = pl.BlockSpec((2, 1, PIECE, C), lambda b: (0, b, 0, 0))
    return pl.pallas_call(
        feed_kernel,
        grid=(batch,),
        in_specs=[
            pl.BlockSpec((1, 12, 12, ZL, C), lambda b: (b, 0, 0, 0, 0)),
            piece,
            piece,
            piece,
            piece,
            full((C, FFN)),
            full((FFN, C)),
            full((4 * C, 2 * C)),
        ],
        out_specs=pl.BlockSpec((1, 6, 6, ZL, 2 * C), lambda b: (b, 0, 0, 0, 0)),
        out_shape=jax.ShapeDtypeStruct((batch, 6, 6, ZL, 2 * C), BF),
        scratch_shapes=[pltpu.VMEM((12, 12, ZL, C), F32)],
        cost_estimate=pl.CostEstimate(flops=14_000_000_000, bytes_accessed=14_000_000, transcendentals=7_000_000),
        compiler_params=pltpu.CompilerParams(vmem_limit_bytes=60 << 20),
        name="feed",
    )(tok, first, mid_a, mid_b, last, w_up, w_down, w_merge)


def on_device(tokens, w_qkv, w_proj, w_up, w_down, w_merge, earth_bias, position_index, region_ids):
    tok = jnp.transpose(tokens, (0, 2, 3, 1, 4))
    order = window_order()
    (
        bias, mid_left, mid_right, last_left, last_right, below_left, below_right,
        next_last, prev_last, next_below, prev_below,
    ) = gather(tok, earth_bias, position_index, region_ids)
    last_out, below_out, next_mid, prev_mid = attend(
        [
            (array, None, 0)
            for array in (
                last_left, below_left, last_right, below_right, next_last, next_below, prev_last, prev_below
            )
        ],
        order, w_qkv, w_proj, bias, 1, (mid_left, mid_right),
    )
    mid_a, mid_b = attend(
        [(array, 1, piece) for array in (mid_left, mid_right, next_mid, prev_mid) for piece in range(2)],
        order, w_qkv, w_proj, bias, 0,
    )
    first_out = passed_along(below_out, "lat", 1)
    merged = feed(tok, first_out, mid_a, mid_b, last_out, w_up, w_down, w_merge)
    return jnp.transpose(merged, (0, 3, 1, 2, 4))


def solution(mesh):
    in_specs = (
        P(None, None, "lat", "lon", None),
        P(),
        P(),
        P(),
        P(),
        P(),
        P("lat", None, None, None),
        P(),
        P("lat", None, None),
    )
    out_specs = P(None, None, "lat", "lon", None)
    return jax.shard_map(
        on_device, mesh=mesh, in_specs=in_specs, out_specs=out_specs, check_vma=False
    )
```

profile of v0, /device:TPU:1, one launch (start us, length us, event | category | flops | bytes accessed | tf_op | source)
XLA Modules:
  0.0 137.2 jit_solution(6392359572732276530)
XLA Ops:
  0.0 1.3 reshape.3.labels_ref
  1.3 51.6 %gather.1 = (f32[18,96,8,256]{3,2,1,0:T(8,128)}, bf16[4,2,144,384]{3,2,1,0:T(8,128)(2,1)}, bf16[4,2,144,384]{3,2,1,0:T(8,128)(2,1)}, bf16[4,144,384]{2,1,0:T(8,1...) custom-call(s32[144,144]{1,0:T(8,128)} %index_ref.1, ...), custom_call_target="tpu_custom_call" | custom-call | flops 20000000 | bytes 100000000 | tf_op jit(solution)/shard_map/gather/pallas_call | solution.py:208
  52.9 30.7 %attend.2 = (bf16[2,4,144,384]{3,2,1,0:T(8,128)(2,1)}, bf16[2,4,144,384]{3,2,1,0:T(8,128)(2,1)}, bf16[4,2,144,384]{3,2,1,0:T(8,128)(2,1)}, bf16[4,2,144,384]{3,2,1,0:T(8,128)(2,1)}) custom-call(bf16[4,144,384]{2,1,0:T(8,128)(2,1)} %get-tuple-element.22.lower_a, bf16[4,144,384]{2,1,0:T(8,128)(2,1)} %get-tuple-element.23.lower_b, ...), custom_call_target="tpu_custom_call" | custom-call | flops 20000000000 | bytes 16000000 | tf_op jit(solution)/shard_map/attend/pallas_call | solution.py:333
  83.7 1.9 %collective-permute-start = (bf16[2,4,144,384]{3,2,1,0:T(8,128)(2,1)}, bf16[2,4,144,384]{3,2,1,0:T(8,128)(2,1)S(1)}, u32[]{:S(2)}, u32[]{:S(2)}) collective-permute-start(bf16[2,4,144,384]{3,2,1,0:T(8,128)(2,1)} %get-tuple-element.33), channel_id=1, source_target_pairs={{96,0},{0,32},{32,64},{64,96},{97,1},{1,33},{33,65},{65,97},{98,2}... | collective-permute-start | bytes 2654216 | tf_op jit(solution)/shard_map/ppermute | solution.py:28
  85.6 23.4 %attend.3 = (bf16[2,4,144,384]{3,2,1,0:T(8,128)(2,1)}, bf16[2,4,144,384]{3,2,1,0:T(8,128)(2,1)}) custom-call(bf16[4,2,144,384]{3,2,1,0:T(8,128)(2,1)} %get-tuple-element.31.rest_2_.lower_a.lower_b, bf16[4,2,144,384]{3,2,1,0:T(8,128)(2,1)} %get-tuple-element.31.rest_2_.lower_a.lower_b, bf16[4,2,144,384]{3,2,1,0:T(8,128)(2,1)} %get-tuple-element.32.rest_3_.upper_a.upper_b, ...), custom_call_target="tpu_custom_call" | custom-call | flops 20000000000 | bytes 16000000 | tf_op jit(solution)/shard_map/attend/pallas_call | solution.py:333
  109.0 0.0 collective-permute-done.first_ref
  109.0 0.0 copy-start
  109.0 0.9 copy-done
  109.9 27.3 %feed.1 = bf16[4,6,6,8,768]{4,3,2,1,0:T(8,128)(2,1)} custom-call(bf16[4,12,12,8,384]{4,3,2,1,0:T(8,128)(2,1)} %bitcast.4, bf16[2,4,144,384]{3,2,1,0:T(8,128)(2,1)} %copy-done, bf16[2,4,144,384]{3,2,1,0:T(8,128)(2,1)} %get-tuple-element.36.mid_a, bf16[2,4,144,384]{3,2,1,0:T(8,128)(2,1)} %get-tuple-element.37.mid_b, ...), custom_call_target="tpu_custom_call" | custom-call | flops 14000000000 | bytes 14000000 | tf_op jit(solution)/shard_map/feed/pallas_call | solution.py:387
Async XLA Ops:
  83.7 25.3 %collective-permute-start = (bf16[2,4,144,384]{3,2,1,0:T(8,128)(2,1)}, bf16[2,4,144,384]{3,2,1,0:T(8,128)(2,1)S(1)}, u32[]{:S(2)}, u32[]{:S(2)}) collective-permute-start(bf16[2,4,144,384]{3,2,1,0:T(8,128)(2,1)} %get-tuple-element.33), channel_id=1, source_target_pairs={{96,0},{0,32},{32,64},{64,96},{97,1},{1,33},{33,65},{65,97},{98,2}... | collective-permute-start | bytes 2654216 | tf_op jit(solution)/shard_map/ppermute | solution.py:28
  109.0 0.9 copy-start
where the time goes:
time: 137 us
  Pallas kernels  133 us (97%)
  local copies, waits for them, and re-layouts  2.22 us (2%)
  starting transfers between devices  1.9 us (1%)
    pallas_call x2, Pallas kernels, attend(): pl.pallas_call(attend_kernel, grid=(batch,), in_specs=specs + [full((CELL...  54.2 us
    pallas_call x1, Pallas kernels, gather(): pl.pallas_call(gather_kernel, grid=(STEPS,), in_specs=[pl.BlockSpec(memor...  51.6 us
    pallas_call x1, Pallas kernels, feed(): pl.pallas_call(feed_kernel, grid=(batch,), in_specs=[pl.BlockSpec((1, 12,...  27.3 us
  transfers between devices with their start and end apart: 1, of which 0 were waited for; matrix products, arithmetic and copies ran while one was open for 0% of the time, Pallas kernels for 17%

commit v1 on v0

--- a/solution.py
+++ b/solution.py
@@ -28,16 +28,6 @@
     return lax.ppermute(block, axis, route)
 
 
-def window_order():
-    one_hot = np.zeros((CELLS, CELLS), np.float32)
-    for zw in range(ZW):
-        for z in range(2):
-            for r in range(6):
-                for c in range(6):
-                    one_hot[zw * HALF + z * 36 + r * 6 + c, (r * 6 + c) * ZL + (2 * zw + 1 + z) % ZL] = 1.0
-    return one_hot
-
-
 def normalized(x):
     width = x.shape[-1]
     center = x - jnp.sum(x, axis=-1, keepdims=True) * (1.0 / width)
@@ -93,7 +83,7 @@
 
 
 def slot_order():
-    return np.arange(SLOTS, dtype=np.int32).reshape(12, 2, 6).transpose(1, 0, 2).reshape(-1)
+    return np.arange(SLOTS, dtype=np.int32).reshape(2, 6, 2, 6).transpose(2, 1, 3, 0).reshape(-1)
 
 
 def gather_kernel(
@@ -160,14 +150,16 @@
             block(n).wait_recv()
             block(4 + n).start()
 
+    order = [int(n) for n in slot_order()]
+
     def pick(turn, carry):
         for j in range(PICKS):
             row = step * ROWS_AT_ONCE + turn * (PICKS // 2) + j // 2
             side, place = row // HALF, row % HALF
-            slot = (place // 6) * 12 + side * 6 + place % 6
+            slot = place % 2 * 72 + place // 12 * 12 + side * 6 + place // 2 % 6
             base = pl.multiple_of(turn * (PICKS * HALF) + j * HALF, 8)
             for k in range(HALF):
-                picked[pl.ds(base + k, 1), :] = rows[pl.ds(index_ref[slot, j % 2 * 6 + k // 6 * 12 + k % 6], 1), :]
+                picked[pl.ds(base + k, 1), :] = rows[pl.ds(index_ref[slot, order[j % 2 * HALF + k]], 1), :]
         return carry
 
     lax.fori_loop(0, ROWS_AT_ONCE * 2 // PICKS, pick, 0)
@@ -241,7 +233,7 @@
 
 
 def attend_kernel(
-    lower_a, lower_b, upper_a, upper_b, right_a, right_b, left_a, left_b, order_ref, back_ref, w_qkv_ref, w_proj_ref, *rest
+    lower_a, lower_b, upper_a, upper_b, right_a, right_b, left_a, left_b, w_qkv_ref, w_proj_ref, *rest
 ):
     bias_refs, rest = rest[:2], rest[2:]
     if len(rest) > 5:
@@ -262,10 +254,32 @@
     else:
         blocks = None
         out_a, out_b, own_scr, halo_scr, ctx_scr = rest
-    order = order_ref[...]
+    level = lax.broadcasted_iota(jnp.int32, (1, ZL, 128), 1)
+    level = jnp.concatenate([level] * 3, axis=-1)
+
+    def chosen(parts, which):
+        result = parts[0]
+        for n in range(1, 4):
+            result = jnp.where(which == n, parts[n], result)
+        return result
 
     def windows(top, bottom):
-        return dot(order, jnp.concatenate([top, bottom], axis=0)).astype(BF)
+        x = jnp.concatenate([top, bottom], axis=0).astype(F32).reshape(9, 4, ZL, C)
+        result = []
+        for zw in range(ZW):
+            parts = [pltpu.roll(x[:, i], (2 * i - 2 * zw - 1) % ZL, axis=1) for i in range(4)]
+            result.append(chosen(parts, level // 2).reshape(HALF, C))
+        return jnp.concatenate(result, axis=0).astype(BF)
+
+    def natural(x):
+        result = []
+        for i in range(4):
+            parts = [
+                pltpu.roll(x[zw * HALF : (zw + 1) * HALF].reshape(9, ZL, C), (2 * zw + 1 - 2 * i) % ZL, axis=1)
+                for zw in range(ZW)
+            ]
+            result.append(chosen(parts, (level + ZL - 1) % ZL // 2))
+        return jnp.stack(result, axis=1).reshape(CELLS, C)
 
     own = jnp.concatenate([windows(upper_a[0], upper_b[0]), windows(lower_a[0], lower_b[0])], axis=0)
     own_scr[...] = dot(own, w_qkv_ref[...])
@@ -300,10 +314,9 @@
                     top = jnp.where(masks[h], both[h * HALF : (h + 1) * HALF, :128], top)
                     total = jnp.where(masks[h], both[h * HALF : (h + 1) * HALF, 128:], total)
                 ctx_scr[rows, lanes] = top / total
-    back = back_ref[...]
     for side in range(2):
-        natural = dot(back, ctx_scr[CELLS * side : CELLS * (side + 1), :].astype(BF)).astype(BF)
-        result = dot(natural, w_proj_ref[...]).astype(BF)
+        context = natural(ctx_scr[CELLS * side : CELLS * (side + 1), :]).astype(BF)
+        result = dot(context, w_proj_ref[...]).astype(BF)
         out_a[1 - side, 0] = result[:PIECE]
         out_b[1 - side, 0] = result[PIECE:]
     if blocks is not None:
@@ -314,7 +327,7 @@
                 block.wait()
 
 
-def attend(streams, order, w_qkv, w_proj, bias, lw, travelling=()):
+def attend(streams, w_qkv, w_proj, bias, lw, travelling=()):
     batch = streams[-1][0].shape[0]
     arrays, specs = [], []
     for array, dim, index in streams:
@@ -335,8 +348,6 @@
         grid=(batch,),
         in_specs=specs
         + [
-            full((CELLS, CELLS)),
-            full((CELLS, CELLS)),
             full((C, 3 * C)),
             full((C, C)),
             pl.BlockSpec((STEPS // 2, ZW * HEADS, ROWS_AT_ONCE, LANES), lambda b: (0, lw, 0, 0)),
@@ -354,7 +365,7 @@
         cost_estimate=pl.CostEstimate(flops=20_000_000_000, bytes_accessed=16_000_000, transcendentals=4_000_000),
         compiler_params=pltpu.CompilerParams(vmem_limit_bytes=60 << 20, **remote_params),
         name="attend",
-    )(*arrays, jnp.asarray(order, BF), jnp.asarray(order.T, BF), w_qkv, w_proj, bias, bias, *travelling)
+    )(*arrays, w_qkv, w_proj, bias, bias, *travelling)
 
 
 CHUNK = 768
@@ -408,7 +419,6 @@
 
 def on_device(tokens, w_qkv, w_proj, w_up, w_down, w_merge, earth_bias, position_index, region_ids):
     tok = jnp.transpose(tokens, (0, 2, 3, 1, 4))
-    order = window_order()
     (
         bias, mid_left, mid_right, last_left, last_right, below_left, below_right,
         next_last, prev_last, next_below, prev_below,
@@ -420,11 +430,11 @@
                 last_left, below_left, last_right, below_right, next_last, next_below, prev_last, prev_below
             )
         ],
-        order, w_qkv, w_proj, bias, 1, (mid_left, mid_right),
+        w_qkv, w_proj, bias, 1, (mid_left, mid_right),
     )
     mid_a, mid_b = attend(
         [(array, 1, piece) for array in (mid_left, mid_right, next_mid, prev_mid) for piece in range(2)],
-        order, w_qkv, w_proj, bias, 0,
+        w_qkv, w_proj, bias, 0,
     )
     first_out = passed_along(below_out, "lat", 1)
     merged = feed(tok, first_out, mid_a, mid_b, last_out, w_up, w_down, w_merge)

time: 137 us -> 134 us (0.978)
  Pallas kernels: 133 us -> 130 us
    pallas_call x2, Pallas kernels: 54.2 us -> 51 us  [attend(): pl.pallas_call(attend_kernel, grid=(batch,), in_specs=specs + [full((C, 3...]
  transfers between devices with their start and end apart: 1 -> 1, of which waited for: 0 -> 0; matrix products, arithmetic and copies ran while one was open for 0% -> 0% of each run, Pallas kernels for 17% -> 15%
where the time goes in v1:
time: 134 us
  Pallas kernels  130 us (97%)
  local copies, waits for them, and re-layouts  2.22 us (2%)
  starting transfers between devices  1.77 us (1%)
    pallas_call x1, Pallas kernels, gather(): pl.pallas_call(gather_kernel, grid=(STEPS,), in_specs=[pl.BlockSpec(memor...  51.8 us
    pallas_call x2, Pallas kernels, attend(): pl.pallas_call(attend_kernel, grid=(batch,), in_specs=specs + [full((C, 3...  51 us
    pallas_call x1, Pallas kernels, feed(): pl.pallas_call(feed_kernel, grid=(batch,), in_specs=[pl.BlockSpec((1, 12,...  27.3 us
  transfers between devices with their start and end apart: 1, of which 0 were waited for; matrix products, arithmetic and copies ran while one was open for 0% of the time, Pallas kernels for 15%

profile of v1, /device:TPU:1, one launch (start us, length us, event | category | flops | bytes accessed | tf_op | source)
XLA Modules:
  0.0 134.0 jit_solution(6179756909342145553)
XLA Ops:
  0.0 1.3 reshape.3.labels_ref
  1.3 51.8 %gather.1 = (f32[18,96,8,256]{3,2,1,0:T(8,128)}, bf16[4,2,144,384]{3,2,1,0:T(8,128)(2,1)}, bf16[4,2,144,384]{3,2,1,0:T(8,128)(2,1)}, bf16[4,144,384]{2,1,0:T(8,1...) custom-call(s32[144,144]{1,0:T(8,128)} %index_ref.1, ...), custom_call_target="tpu_custom_call" | custom-call | flops 20000000 | bytes 100000000 | tf_op jit(solution)/shard_map/gather/pallas_call | solution.py:200
  53.1 30.9 %attend.2 = (bf16[2,4,144,384]{3,2,1,0:T(8,128)(2,1)}, bf16[2,4,144,384]{3,2,1,0:T(8,128)(2,1)}, bf16[4,2,144,384]{3,2,1,0:T(8,128)(2,1)}, bf16[4,2,144,384]{3,2,1,0:T(8,128)(2,1)}) custom-call(bf16[4,144,384]{2,1,0:T(8,128)(2,1)} %get-tuple-element.22.lower_a, bf16[4,144,384]{2,1,0:T(8,128)(2,1)} %get-tuple-element.23.lower_b, ...), custom_call_target="tpu_custom_call" | custom-call | flops 20000000000 | bytes 16000000 | tf_op jit(solution)/shard_map/attend/pallas_call | solution.py:346
  84.0 1.8 %collective-permute-start = (bf16[2,4,144,384]{3,2,1,0:T(8,128)(2,1)}, bf16[2,4,144,384]{3,2,1,0:T(8,128)(2,1)S(1)}, u32[]{:S(2)}, u32[]{:S(2)}) collective-permute-start(bf16[2,4,144,384]{3,2,1,0:T(8,128)(2,1)} %get-tuple-element.33), channel_id=1, source_target_pairs={{96,0},{0,32},{32,64},{64,96},{97,1},{1,33},{33,65},{65,97},{98,2}... | collective-permute-start | bytes 2654216 | tf_op jit(solution)/shard_map/ppermute | solution.py:28
  85.8 20.1 %attend.3 = (bf16[2,4,144,384]{3,2,1,0:T(8,128)(2,1)}, bf16[2,4,144,384]{3,2,1,0:T(8,128)(2,1)}) custom-call(bf16[4,2,144,384]{3,2,1,0:T(8,128)(2,1)} %get-tuple-element.31.rest_2_.lower_a.lower_b, bf16[4,2,144,384]{3,2,1,0:T(8,128)(2,1)} %get-tuple-element.31.rest_2_.lower_a.lower_b, bf16[4,2,144,384]{3,2,1,0:T(8,128)(2,1)} %get-tuple-element.32.rest_3_.upper_a.upper_b, ...), custom_call_target="tpu_custom_call" | custom-call | flops 20000000000 | bytes 16000000 | tf_op jit(solution)/shard_map/attend/pallas_call | solution.py:346
  105.8 0.0 collective-permute-done.first_ref
  105.9 0.0 copy-start
  105.9 0.9 copy-done
  106.8 27.3 %feed.1 = bf16[4,6,6,8,768]{4,3,2,1,0:T(8,128)(2,1)} custom-call(bf16[4,12,12,8,384]{4,3,2,1,0:T(8,128)(2,1)} %bitcast.4, bf16[2,4,144,384]{3,2,1,0:T(8,128)(2,1)} %copy-done, bf16[2,4,144,384]{3,2,1,0:T(8,128)(2,1)} %get-tuple-element.36.mid_a, bf16[2,4,144,384]{3,2,1,0:T(8,128)(2,1)} %get-tuple-element.37.mid_b, ...), custom_call_target="tpu_custom_call" | custom-call | flops 14000000000 | bytes 14000000 | tf_op jit(solution)/shard_map/feed/pallas_call | solution.py:398
Async XLA Ops:
  84.0 21.9 %collective-permute-start = (bf16[2,4,144,384]{3,2,1,0:T(8,128)(2,1)}, bf16[2,4,144,384]{3,2,1,0:T(8,128)(2,1)S(1)}, u32[]{:S(2)}, u32[]{:S(2)}) collective-permute-start(bf16[2,4,144,384]{3,2,1,0:T(8,128)(2,1)} %get-tuple-element.33), channel_id=1, source_target_pairs={{96,0},{0,32},{32,64},{64,96},{97,1},{1,33},{33,65},{65,97},{98,2}... | collective-permute-start | bytes 2654216 | tf_op jit(solution)/shard_map/ppermute | solution.py:28
  105.9 0.9 copy-start
